TPU v7x, 32 devices: a whole 2x2x4 slice. The times are simulated.
32 devices in a mesh: row: 16 (over z, y, x), col: 2 (over core).
Axes of the slice: x: 2, y: 2, z: 4, core: 2. Of those that a mesh axis runs over, the one named last changes fastest.
Arguments:
- right_side: float32 [12288, 1280], P('row', 'col'), may hold values from -6 to 6
- factor_panel: bfloat16 [512, 3, 12288], P('col', None, 'row'), may hold values from -0.15625 to 0.15625
- diag_inverse: float32 [3, 512, 512], P(None, 'row'), may hold values from -1.5 to 1.5, as said below
Outputs:
- solved: float32 [12288, 1280], P('row', 'col')
Inputs may be any that keep to these rules, and one draw needn't show every extreme that they name: `diag_inverse`: each of the 3 blocks is zero above its diagonal; its diagonal lies between 0.5 and 1.5.
All inputs are finite; a program needn't handle non-finite values.
Results may differ from a plain program's by a relative error of at most 0.003.
Values may be sent and summed in bfloat16 or wider, within the bound.
A program may use at most 64 MiB of HBM per device.

v0:
```python
import jax
import jax.numpy as jnp
from jax import lax
from jax.sharding import PartitionSpec as P

KB = 3


def shards(right_side, factor_panel, diag_inverse):
    local_rows = right_side.shape[0]
    block_rows = diag_inverse.shape[1]
    workspace = right_side
    for step_index in reversed(range(KB)):
        offset = local_rows - (KB - step_index) * block_rows
        block_rhs = workspace[offset : offset + block_rows]
        partial_value = lax.dot_general(
            diag_inverse[step_index],
            block_rhs,
            (((0,), (0,)), ((), ())),
            precision=lax.Precision.HIGHEST,
            preferred_element_type=jnp.float32,
        )
        whole_x = lax.psum(partial_value, "row")
        own_rows = lax.dynamic_slice_in_dim(
            whole_x, lax.axis_index("row") * block_rows, block_rows, 0
        )
        block_low = whole_x.astype(jnp.bfloat16)
        update = lax.dot_general(
            lax.all_gather(factor_panel[:, step_index, :offset], "col", axis=0, tiled=True),
            block_low,
            (((0,), (0,)), ((), ())),
            preferred_element_type=jnp.float32,
        )
        workspace = jnp.concatenate(
            [workspace[:offset] - update, own_rows, workspace[offset + block_rows :]], axis=0
        )
    return workspace


def solution(mesh):
    placed = (P("row", "col"), P("col", None, "row"), P(None, "row", None))
    return jax.shard_map(
        shards, mesh=mesh, in_specs=placed, out_specs=P("row", "col"), check_vma=False
    )
```

profile of v0, /device:TPU:0, one launch (start us, length us, event | category | flops | bytes accessed | tf_op | source)
XLA Modules:
  0.0 380.1 jit_solution(885599477888310501)
XLA Ops:
  6.5 0.0 all-reduce.4.cloned.1.call-start
  6.5 3.2 fusion.8
  9.8 0.0 all-reduce.4.cloned.1.call-update
  9.8 0.0 all-reduce.6.cloned.1.call-start
  9.8 1.0 slice.39
  10.9 2.4 all-gather
  13.3 0.0 copy-start.2
  13.3 117.0 %all-reduce.4.cloned.1.call-done = f32[512,640]{1,0:T(8,128)} async-done(((f32[512,640]{1,0:T(8,128)}), f32[512,640]{1,0:T(8,128)}) %all-reduce.4.cloned.1.call-update) | async-done | bytes 1310736 | tf_op jit(solution)/shard_map/psum | solution.py:23
  130.3 2.7 bitcast_subtract_fusion
  133.0 0.0 copy-done.2
  133.0 2.3 convolution_bitcast_fusion.1
  135.3 0.0 all-reduce.6.cloned.1.call-update
  135.3 0.0 all-reduce.8.cloned.1.call-start
  135.4 1.0 slice.43
  136.4 2.4 all-gather.1
  138.7 111.2 %all-reduce.6.cloned.1.call-done = f32[512,640]{1,0:T(8,128)} async-done(((f32[512,640]{1,0:T(8,128)}), f32[512,640]{1,0:T(8,128)}) %all-reduce.6.cloned.1.call-update) | async-done | bytes 1310736 | tf_op jit(solution)/shard_map/psum | solution.py:23
  249.9 2.1 slice_subtract_fusion
  252.1 0.0 copy-start
  252.1 1.2 copy-done
  253.3 2.3 convolution_bitcast_fusion
  255.6 0.0 copy-start.1
  255.6 0.0 all-reduce.8.cloned.1.call-update
  255.6 1.2 slice.47
  256.8 2.4 all-gather.2
  259.1 0.9 constant_dynamic-slice_fusion
  260.1 0.9 constant_dynamic-slice_fusion.1
  261.0 108.2 %all-reduce.8.cloned.1.call-done = f32[512,640]{1,0:T(8,128)} async-done(((f32[512,640]{1,0:T(8,128)}), f32[512,640]{1,0:T(8,128)}) %all-reduce.8.cloned.1.call-update) | async-done | bytes 1310736 | tf_op jit(solution)/shard_map/psum | solution.py:23
  369.2 0.9 constant_dynamic-slice_fusion.2
  370.1 0.0 copy-done.1
  370.1 2.1 slice_subtract_fusion.1
  372.2 1.4 pad_maximum_fusion
Async XLA Ops:
  6.5 123.7 %all-reduce.4.cloned.1.call-start = ((), (), s32[]{:S(2)}) async-start(), calls=%async_computation | async-start | bytes 2621440 | tf_op jit(solution)/shard_map/psum | solution.py:23
  9.8 240.2 %all-reduce.6.cloned.1.call-start = ((), (), s32[]{:S(2)}) async-start(), calls=%async_computation.1 | async-start | bytes 2621440 | tf_op jit(solution)/shard_map/psum | solution.py:23
  13.3 119.7 %copy-start.2 = (f32[3,32,512]{2,1,0:T(8,128)S(1)}, f32[3,32,512]{2,1,0:T(8,128)}, u32[]{:S(2)}) copy-start(f32[3,32,512]{2,1,0:T(8,128)} %param.5) | copy-start | bytes 589828
  135.3 233.9 %all-reduce.8.cloned.1.call-start = ((), (), s32[]{:S(2)}) async-start(), calls=%async_computation.2 | async-start | bytes 2621440 | tf_op jit(solution)/shard_map/psum | solution.py:23
  252.1 1.2 copy-start
  255.6 114.5 %copy-start.1 = (f32[704,640]{1,0:T(8,128)S(1)}, f32[704,640]{1,0:T(8,128)}, u32[]{:S(2)}) copy-start(f32[704,640]{1,0:T(8,128)} %copy-done) | copy-start | bytes 5406724
Sparse Core Ops, SparseCore 0:
  12.8 117.4 all-reduce.3
  136.5 113.3 all-reduce.5
  255.7 113.4 all-reduce.7
where the time goes:
time: 381 us; the launch traced here: 380 us
  waiting for transfers between devices  336 us (88%)
  matrix products  14.7 us (4%)
  between operations  13.2 us (3%)
  blocking collectives  7.18 us (2%)
  local copies, waits for them, and re-layouts  7.14 us (2%)
    psum x3, waiting for transfers between devices, shards(): whole_x = lax.psum(partial_value, 'row')  336 us
    dot_general x3, matrix products, shards(): lax.dot_general(diag_inverse[step_index], block_rhs, (((0,), (0,)), ((),...  7.79 us
  transfers between devices with their start and end apart: 3, of which 3 were waited for; matrix products, arithmetic and copies ran while one was open for 1% of the time, Pallas kernels for 0%

commit v1 on v0

--- a/solution.py
+++ b/solution.py
@@ -1,9 +1,16 @@
+import functools
+
 import jax
 import jax.numpy as jnp
 from jax import lax
+from jax.experimental import pallas as pl
+from jax.experimental.pallas import tpu as pltpu
 from jax.sharding import PartitionSpec as P
 
 KB = 3
+MESH = pl.DeviceIdType.MESH
+LANES = 128
+PAIRS = ((2, 1), (2, 0), (1, 0))
 
 
 def shards(right_side, factor_panel, diag_inverse):
@@ -37,8 +44,290 @@
     return workspace
 
 
+def nt_dot(left, right):
+    return lax.dot_general(
+        left, right, (((1,), (1,)), ((), ())), preferred_element_type=jnp.float32
+    )
+
+
+def kernel(
+    outer, inner,
+    rhs_ref, ft_ref, dinv_ref, out_ref,
+    ftx, dg, fg, xg, xt, bts, btr, yts, ytr,
+    s1_send, s1_recv, s2_send, s2_recv, sib_send, sib_recv, a2a_send, a2a_recv,
+):
+    n_row = outer * inner
+    me = lax.axis_index("row")
+    core = lax.axis_index("col")
+    z, p = me // inner, me % inner
+    rows, _ = rhs_ref.shape
+    block = dinv_ref.shape[1]
+    half = ft_ref.shape[2]
+    chunk = bts.shape[1]
+    kept = rows - KB * block
+    window = rows - LANES
+
+    barrier = pltpu.get_barrier_semaphore()
+    for d in range(1, n_row):
+        pl.semaphore_signal(
+            barrier, inc=1, device_id={"row": lax.rem(me + d, n_row)}, device_id_type=MESH
+        )
+    pl.semaphore_signal(barrier, inc=1, device_id={"col": 1 - core}, device_id_type=MESH)
+
+    lanes = pl.ds(pl.multiple_of(core * half, half), half)
+    for k in range(KB):
+        dg[core, k, z, p] = dinv_ref[k, :, lanes]
+    for pair, (k, j) in enumerate(PAIRS):
+        fg[core, pair, z, p] = ft_ref[k, kept + j * block : kept + (j + 1) * block, :]
+    bts[...] = rhs_ref[window:, :].T.reshape(n_row, chunk, LANES)
+    btr[me] = bts[me]
+
+    pl.semaphore_wait(barrier, n_row)
+
+    pending = []
+
+    def remote(src, dst, send_sem, recv_sem, device_id):
+        return pltpu.make_async_remote_copy(
+            src_ref=src, dst_ref=dst, send_sem=send_sem, recv_sem=recv_sem,
+            device_id=device_id, device_id_type=MESH,
+        )
+
+    def view(item):
+        kind, i = item
+        if kind == "d":
+            return i, dg.at[core, i]
+        if kind == "f":
+            return KB + i, fg.at[core, i]
+        return 2 * KB + i, xg.at[i]
+
+    def first(item):
+        n, ref = view(item)
+        copies = []
+        for d in range(1, outer):
+            c = remote(
+                ref.at[z, p], ref.at[z, p], s1_send.at[n, d], s1_recv.at[n, d],
+                {"row": lax.rem(z + d, outer) * inner + p},
+            )
+            c.start()
+            pending.append(c)
+            copies.append(c)
+        return copies
+
+    def second(item, copies):
+        for c in copies:
+            c.wait_recv()
+        n, ref = view(item)
+        copies = []
+        for d in range(1, inner):
+            c = remote(
+                ref.at[:, p], ref.at[:, p], s2_send.at[n, d], s2_recv.at[n, d],
+                {"row": z * inner + lax.rem(p + d, inner)},
+            )
+            c.start()
+            pending.append(c)
+            copies.append(c)
+        return copies
+
+    def to_sibling(item, copies):
+        for c in copies:
+            c.wait_recv()
+        n, ref = view(item)
+        c = remote(ref, ref, sib_send.at[n], sib_recv.at[n], {"col": 1 - core})
+        c.start()
+        pending.append(c)
+        return c
+
+    def all_to_all(src, dst, which):
+        copies = []
+        for d in range(1, n_row):
+            to = lax.rem(me + d, n_row)
+            c = remote(
+                src.at[to], dst.at[me], a2a_send.at[which, d], a2a_recv.at[which, d], {"row": to}
+            )
+            c.start()
+            pending.append(c)
+            copies.append(c)
+        return copies
+
+    order = [("d", 2), ("f", 0), ("d", 1), ("f", 1), ("f", 2), ("d", 0)]
+    arrive = {}
+    arrive[order[0]] = first(order[0])
+    b_copies = all_to_all(bts, btr, 0)
+    for item in order[1:]:
+        arrive[item] = first(item)
+    ft_copy = remote(
+        ft_ref, ftx, sib_send.at[2 * KB], sib_recv.at[2 * KB], {"col": 1 - core}
+    )
+    ft_copy.start()
+    pending.append(ft_copy)
+
+    lane_group = lax.broadcasted_iota(jnp.int32, (chunk, LANES), 1) // block
+    per_tile = LANES // block
+
+    def gathered_rhs(k):
+        tiles = []
+        for g in range(n_row // per_tile):
+            total = jnp.zeros((chunk, LANES), jnp.float32)
+            for q in range(per_tile):
+                shift = (block * q - (LANES - (KB - k) * block)) % LANES
+                part = btr[per_tile * g + q]
+                if shift:
+                    part = pltpu.roll(part, shift, 1)
+                total = jnp.where(lane_group == q, part, total)
+            tiles.append(total)
+        return jnp.concatenate(tiles, axis=1)
+
+    def solve(k, w):
+        halves = []
+        for h in range(2):
+            halves.append(
+                jnp.dot(
+                    w, dg[h, k].reshape(n_row * block, half),
+                    precision=lax.Precision.HIGHEST, preferred_element_type=jnp.float32,
+                )
+            )
+        xg[k, z, p] = jnp.concatenate(halves, axis=0).astype(jnp.bfloat16)
+        return halves
+
+    def couple(pair, halves):
+        total = None
+        for h in range(2):
+            term = nt_dot(
+                halves[h].astype(jnp.bfloat16), fg[h, pair].reshape(n_row * block, half)
+            )
+            total = term if total is None else total + term
+        return total
+
+    for item in order[:3]:
+        arrive[item] = second(item, arrive[item])
+    sib = {}
+    sib[order[0]] = to_sibling(order[0], arrive[order[0]])
+    for item in order[3:]:
+        arrive[item] = second(item, arrive[item])
+    for c in b_copies:
+        c.wait_recv()
+    w2 = gathered_rhs(2)
+    w1 = gathered_rhs(1)
+    w0 = gathered_rhs(0)
+    sib[order[0]].wait_recv()
+    x2 = solve(2, w2)
+    a2 = first(("x", 2))
+    for item in order[1:3]:
+        sib[item] = to_sibling(item, arrive[item])
+    sib[("f", 0)].wait_recv()
+    w1 = w1 - couple(0, x2)
+    sib[("d", 1)].wait_recv()
+    x1 = solve(1, w1)
+    a1 = first(("x", 1))
+    a2 = second(("x", 2), a2)
+    for item in order[3:]:
+        sib[item] = to_sibling(item, arrive[item])
+    sib[("f", 1)].wait_recv()
+    w0 = w0 - couple(1, x2)
+    sib[("f", 2)].wait_recv()
+    w0 = w0 - couple(2, x1)
+    sib[("d", 0)].wait_recv()
+    x0 = solve(0, w0)
+    a0 = first(("x", 0))
+
+    whole = [jnp.concatenate(x, axis=1) for x in (x0, x1, x2)]
+    for r in range(n_row):
+        g, q = r // per_tile, r % per_tile
+        total = jnp.zeros((chunk, LANES), jnp.float32)
+        for k in range(KB):
+            start = LANES - (KB - k) * block
+            part = whole[k][:, g * LANES : (g + 1) * LANES]
+            shift = (start - block * q) % LANES
+            if shift:
+                part = pltpu.roll(part, shift, 1)
+            total = jnp.where(lane_group == start // block, part, total)
+        yts[r] = total
+    ytr[me] = yts[me]
+    a1 = second(("x", 1), a1)
+    y_copies = all_to_all(yts, ytr, 1)
+    a0 = second(("x", 0), a0)
+
+    tiles = 3
+    tile = kept // tiles
+
+    def update(k, copies, base):
+        for c in copies:
+            c.wait_recv()
+        v = xg[k].reshape(n_row, 2 * chunk, half).astype(jnp.float32)
+        for h in range(2):
+            xt[h] = v[:, h * chunk : (h + 1) * chunk].reshape(n_row * chunk, half).astype(
+                jnp.bfloat16
+            )
+
+        @pl.loop(0, tiles)
+        def _(t):
+            at = pl.ds(pl.multiple_of(t * tile, tile), tile)
+            out_ref[at, :] = (
+                base[at, :] - nt_dot(ft_ref[k, at, :], xt[core]) - nt_dot(ftx[k, at, :], xt[1 - core])
+            )
+
+    ft_copy.wait_recv()
+    update(2, a2, rhs_ref)
+    update(1, a1, out_ref)
+    update(0, a0, out_ref)
+    for c in y_copies:
+        c.wait_recv()
+    out_ref[kept:, :] = ytr[...].reshape(n_row * chunk, LANES).T[LANES - KB * block :, :]
+    for c in pending:
+        c.wait_send()
+
+
+def fused(outer, inner, right_side, factor_panel, diag_inverse):
+    rows, columns = right_side.shape
+    half = factor_panel.shape[0]
+    block = diag_inverse.shape[1]
+    n_row = outer * inner
+    chunk = columns // n_row
+    panel = jnp.transpose(factor_panel, (1, 2, 0))
+    vmem = pl.BlockSpec(memory_space=pltpu.VMEM)
+    dma = pltpu.SemaphoreType.DMA
+    square = (2, KB, outer, inner, block, half)
+    return pl.pallas_call(
+        functools.partial(kernel, outer, inner),
+        out_shape=jax.ShapeDtypeStruct((rows, columns), jnp.float32),
+        in_specs=[vmem] * 3,
+        out_specs=vmem,
+        scratch_shapes=[
+            pltpu.VMEM((KB, rows, half), jnp.bfloat16),
+            pltpu.VMEM(square, jnp.float32),
+            pltpu.VMEM(square, jnp.bfloat16),
+            pltpu.VMEM((KB, outer, inner, 2 * chunk, half), jnp.bfloat16),
+            pltpu.VMEM((2, columns, half), jnp.bfloat16),
+            pltpu.VMEM((n_row, chunk, LANES), jnp.float32),
+            pltpu.VMEM((n_row, chunk, LANES), jnp.float32),
+            pltpu.VMEM((n_row, chunk, LANES), jnp.float32),
+            pltpu.VMEM((n_row, chunk, LANES), jnp.float32),
+            dma((3 * KB, outer)),
+            dma((3 * KB, outer)),
+            dma((3 * KB, inner)),
+            dma((3 * KB, inner)),
+            dma((2 * KB + 1,)),
+            dma((2 * KB + 1,)),
+            dma((2, n_row)),
+            dma((2, n_row)),
+        ],
+        compiler_params=pltpu.CompilerParams(
+            collective_id=0, has_side_effects=True, vmem_limit_bytes=48 * 1024 * 1024
+        ),
+        cost_estimate=pl.CostEstimate(
+            flops=2 * KB * rows * columns * 2 * half, bytes_accessed=8 * rows * columns,
+            transcendentals=0,
+        ),
+    )(right_side, panel, diag_inverse)
+
+
 def solution(mesh):
+    n_row, n_col = mesh.shape["row"], mesh.shape["col"]
+    inner = 4
     placed = (P("row", "col"), P("col", None, "row"), P(None, "row", None))
+    body = shards
+    if n_col == 2 and n_row == 16:
+        body = functools.partial(fused, n_row // inner, inner)
     return jax.shard_map(
-        shards, mesh=mesh, in_specs=placed, out_specs=P("row", "col"), check_vma=False
+        body, mesh=mesh, in_specs=placed, out_specs=P("row", "col"), check_vma=False
     )

time: 381 us -> 75.2 us (0.20)
  waiting for transfers between devices: 336 us -> 0 us
  Pallas kernels: 0 us -> 71.7 us
  matrix products: 14.7 us -> 0 us
  between operations: 13.2 us -> 0.03 us
  blocking collectives: 7.18 us -> 0 us
  local copies, waits for them, and re-layouts: 7.14 us -> 3.27 us
    psum x3 -> x0, waiting for transfers between devices: 336 us -> none  [shards(): whole_x = lax.psum(partial_value, 'row')]
    pallas_call x0 -> x1, Pallas kernels: none -> 71.7 us  [fused(): pl.pallas_call(functools.partial(kernel, outer, inner), out_shape=jax.Sha...]
    dot_general x6 -> x0, matrix products: 14.7 us -> none  [the longest x3 7.79 us: shards(): lax.dot_general(diag_inverse[step_index], block_rhs, (((0,), (0,)), ((),...]
    all_gather x3 -> x0, blocking collectives: 7.18 us -> none  [shards(): lax.all_gather(factor_panel[:, step_index, :offset], 'col', axis=0, tiled...]
  transfers between devices with their start and end apart: 3 -> 0, of which waited for: 3 -> 0; matrix products, arithmetic and copies ran while one was open for 1% -> 0% of each run, Pallas kernels for 0% -> 0%
where the time goes in v1:
time: 75.2 us; the launch traced here: 75 us
  Pallas kernels  71.7 us (95%)
  local copies, waits for them, and re-layouts  3.27 us (4%)
    pallas_call x1, Pallas kernels, fused(): pl.pallas_call(functools.partial(kernel, outer, inner), out_shape=jax.Sha...  71.7 us
    unnamed x6, local copies, waits for them, and re-layouts  3.27 us

profile of v1, /device:TPU:0, one launch (start us, length us, event | category | flops | bytes accessed | tf_op | source)
XLA Modules:
  0.0 75.0 jit_solution(3681392275460326389)
XLA Ops:
  0.0 0.0 copy-start.1
  0.0 0.0 copy-start
  0.0 1.7 %copy.4 = bf16[256,3,768]{0,2,1:T(8,128)(2,1)S(1)} copy(bf16[256,3,768]{2,0,1:T(8,128)(2,1)} %param.4) | data formatting | bytes 2359296 | tf_op args[1]
  1.7 0.0 copy-done.1
  1.7 0.3 copy-done
  2.0 71.7 %shard_map.37 = f32[768,640]{1,0:T(8,128)S(1)} custom-call(f32[768,640]{1,0:T(8,128)S(1)} %copy-done, bf16[3,768,256]{2,1,0:T(8,128)(2,1)S(1)} %bitcast.1, f32[3,32,512]{2,1,0:T(8,128)S(1)} %copy-done.1), custom_call_target="tpu_custom_call" | custom-call | flops 1509949440 | bytes 3932160 | tf_op jit(solution)/shard_map/pallas_call | solution.py:290
  73.8 1.3 %copy.6 = f32[768,640]{1,0:T(8,128)} copy(f32[768,640]{1,0:T(8,128)S(1)} %shard_map.37) | data formatting | bytes 3932160
Async XLA Ops:
  0.0 1.7 %copy-start.1 = (f32[3,32,512]{2,1,0:T(8,128)S(1)}, f32[3,32,512]{2,1,0:T(8,128)}, u32[]{:S(2)}) copy-start(f32[3,32,512]{2,1,0:T(8,128)} %dinv_ref.1) | copy-start | bytes 589828
  0.0 2.0 %copy-start = (f32[768,640]{1,0:T(8,128)S(1)}, f32[768,640]{1,0:T(8,128)}, u32[]{:S(2)}) copy-start(f32[768,640]{1,0:T(8,128)} %rhs_ref.1) | copy-start | bytes 5898244

commit v2 on v1

--- a/solution.py
+++ b/solution.py
@@ -11,6 +11,13 @@
 MESH = pl.DeviceIdType.MESH
 LANES = 128
 PAIRS = ((2, 1), (2, 0), (1, 0))
+UNITS = (
+    ((0, 0), (1, 0)),
+    ((1, 0), (2, 0)),
+    ((2, 0), (3, 0)),
+    ((3, 0), (2, 1)),
+    ((3, 1), (3, 1)),
+)
 
 
 def shards(right_side, factor_panel, diag_inverse):
@@ -53,7 +60,7 @@
 def kernel(
     outer, inner,
     rhs_ref, ft_ref, dinv_ref, out_ref,
-    ftx, dg, fg, xg, xt, bts, btr, yts, ytr,
+    ftx, ds, dg, fg, xg, xt, bts, btr, yts, ytr,
     s1_send, s1_recv, s2_send, s2_recv, sib_send, sib_recv, a2a_send, a2a_recv,
 ):
     n_row = outer * inner
@@ -74,9 +81,11 @@
         )
     pl.semaphore_signal(barrier, inc=1, device_id={"col": 1 - core}, device_id_type=MESH)
 
-    lanes = pl.ds(pl.multiple_of(core * half, half), half)
+    low = pl.ds(pl.multiple_of(core * LANES, LANES), LANES)
+    high = pl.ds(pl.multiple_of((outer - 1 - core) * LANES, LANES), LANES)
     for k in range(KB):
-        dg[core, k, z, p] = dinv_ref[k, :, lanes]
+        ds[k, z, 0] = dinv_ref[k, :, low]
+        ds[k, z, 1] = dinv_ref[k, :, high]
     for pair, (k, j) in enumerate(PAIRS):
         fg[core, pair, z, p] = ft_ref[k, kept + j * block : kept + (j + 1) * block, :]
     bts[...] = rhs_ref[window:, :].T.reshape(n_row, chunk, LANES)
@@ -91,6 +100,11 @@
             src_ref=src, dst_ref=dst, send_sem=send_sem, recv_sem=recv_sem,
             device_id=device_id, device_id_type=MESH,
         )
+
+    along_x = p + 1 - 2 * (p % 2)
+    along_y = p + 2 - 4 * (p // 2)
+    near = along_x * (1 - core) + along_y * core
+    far = along_y * (1 - core) + along_x * core
 
     def view(item):
         kind, i = item
@@ -101,11 +115,13 @@
         return 2 * KB + i, xg.at[i]
 
     def first(item):
+        kind, i = item
         n, ref = view(item)
+        own = ds.at[i, z] if kind == "d" else ref.at[z, p]
         copies = []
         for d in range(1, outer):
             c = remote(
-                ref.at[z, p], ref.at[z, p], s1_send.at[n, d], s1_recv.at[n, d],
+                own, own, s1_send.at[n, d], s1_recv.at[n, d],
                 {"row": lax.rem(z + d, outer) * inner + p},
             )
             c.start()
@@ -113,20 +129,28 @@
             copies.append(c)
         return copies
 
+    def in_plane(item, slot, way, to):
+        n, ref = view(item)
+        c = remote(
+            ref.at[:, slot], ref.at[:, slot], s2_send.at[n, way], s2_recv.at[n, way],
+            {"row": z * inner + to},
+        )
+        c.start()
+        pending.append(c)
+        return c
+
     def second(item, copies):
         for c in copies:
             c.wait_recv()
-        n, ref = view(item)
-        copies = []
-        for d in range(1, inner):
-            c = remote(
-                ref.at[:, p], ref.at[:, p], s2_send.at[n, d], s2_recv.at[n, d],
-                {"row": z * inner + lax.rem(p + d, inner)},
-            )
-            c.start()
-            pending.append(c)
-            copies.append(c)
-        return copies
+        kind, k = item
+        if kind == "d":
+            for u, ((z0, g0), (z1, g1)) in enumerate(UNITS):
+                dg[core, k, u, p] = ds[k, z0 + core * (z1 - z0), g0 + core * (g1 - g0)]
+        return [in_plane(item, p, 0, near), in_plane(item, p, 1, far)]
+
+    def third(item, copies):
+        copies[0].wait_recv()
+        return [copies[1], in_plane(item, near, 2, far)]
 
     def to_sibling(item, copies):
         for c in copies:
@@ -178,14 +202,17 @@
         return jnp.concatenate(tiles, axis=1)
 
     def solve(k, w):
-        halves = []
-        for h in range(2):
-            halves.append(
-                jnp.dot(
-                    w, dg[h, k].reshape(n_row * block, half),
-                    precision=lax.Precision.HIGHEST, preferred_element_type=jnp.float32,
-                )
-            )
+        def group(side, units):
+            part = dg[side, k, units].reshape(-1, LANES)
+            return jnp.dot(
+                w[:, w.shape[1] - part.shape[0] :], part,
+                precision=lax.Precision.HIGHEST, preferred_element_type=jnp.float32,
+            )
+
+        halves = [
+            jnp.concatenate([group(0, slice(0, 4)), group(1, slice(0, 3))], axis=1),
+            jnp.concatenate([group(1, slice(3, 5)), group(0, slice(4, 5))], axis=1),
+        ]
         xg[k, z, p] = jnp.concatenate(halves, axis=0).astype(jnp.bfloat16)
         return halves
 
@@ -198,12 +225,13 @@
             total = term if total is None else total + term
         return total
 
-    for item in order[:3]:
+    for item in order[:2]:
         arrive[item] = second(item, arrive[item])
+    arrive[order[0]] = third(order[0], arrive[order[0]])
+    arrive[order[2]] = second(order[2], arrive[order[2]])
+    arrive[order[1]] = third(order[1], arrive[order[1]])
     sib = {}
     sib[order[0]] = to_sibling(order[0], arrive[order[0]])
-    for item in order[3:]:
-        arrive[item] = second(item, arrive[item])
     for c in b_copies:
         c.wait_recv()
     w2 = gathered_rhs(2)
@@ -212,6 +240,11 @@
     sib[order[0]].wait_recv()
     x2 = solve(2, w2)
     a2 = first(("x", 2))
+    for item in order[3:]:
+        arrive[item] = second(item, arrive[item])
+    for item in order[2:]:
+        arrive[item] = third(item, arrive[item])
+    a2 = second(("x", 2), a2)
     for item in order[1:3]:
         sib[item] = to_sibling(item, arrive[item])
     sib[("f", 0)].wait_recv()
@@ -219,9 +252,10 @@
     sib[("d", 1)].wait_recv()
     x1 = solve(1, w1)
     a1 = first(("x", 1))
-    a2 = second(("x", 2), a2)
     for item in order[3:]:
         sib[item] = to_sibling(item, arrive[item])
+    a2 = third(("x", 2), a2)
+    a1 = second(("x", 1), a1)
     sib[("f", 1)].wait_recv()
     w0 = w0 - couple(1, x2)
     sib[("f", 2)].wait_recv()
@@ -229,6 +263,7 @@
     sib[("d", 0)].wait_recv()
     x0 = solve(0, w0)
     a0 = first(("x", 0))
+    a1 = third(("x", 1), a1)
 
     whole = [jnp.concatenate(x, axis=1) for x in (x0, x1, x2)]
     for r in range(n_row):
@@ -243,7 +278,6 @@
             total = jnp.where(lane_group == start // block, part, total)
         yts[r] = total
     ytr[me] = yts[me]
-    a1 = second(("x", 1), a1)
     y_copies = all_to_all(yts, ytr, 1)
     a0 = second(("x", 0), a0)
 
@@ -268,6 +302,7 @@
 
     ft_copy.wait_recv()
     update(2, a2, rhs_ref)
+    a0 = third(("x", 0), a0)
     update(1, a1, out_ref)
     update(0, a0, out_ref)
     for c in y_copies:
@@ -287,6 +322,7 @@
     vmem = pl.BlockSpec(memory_space=pltpu.VMEM)
     dma = pltpu.SemaphoreType.DMA
     square = (2, KB, outer, inner, block, half)
+    packed = (2, KB, len(UNITS), inner, block, LANES)
     return pl.pallas_call(
         functools.partial(kernel, outer, inner),
         out_shape=jax.ShapeDtypeStruct((rows, columns), jnp.float32),
@@ -294,7 +330,8 @@
         out_specs=vmem,
         scratch_shapes=[
             pltpu.VMEM((KB, rows, half), jnp.bfloat16),
-            pltpu.VMEM(square, jnp.float32),
+            pltpu.VMEM((KB, outer, 2, block, LANES), jnp.float32),
+            pltpu.VMEM(packed, jnp.float32),
             pltpu.VMEM(square, jnp.bfloat16),
             pltpu.VMEM((KB, outer, inner, 2 * chunk, half), jnp.bfloat16),
             pltpu.VMEM((2, columns, half), jnp.bfloat16),
@@ -304,8 +341,8 @@
             pltpu.VMEM((n_row, chunk, LANES), jnp.float32),
             dma((3 * KB, outer)),
             dma((3 * KB, outer)),
-            dma((3 * KB, inner)),
-            dma((3 * KB, inner)),
+            dma((3 * KB, 3)),
+            dma((3 * KB, 3)),
             dma((2 * KB + 1,)),
             dma((2 * KB + 1,)),
             dma((2, n_row)),

time: 75.2 us -> 69.5 us (0.924)
  Pallas kernels: 71.7 us -> 66 us
    pallas_call x1, Pallas kernels: 71.7 us -> 66 us  [fused(): pl.pallas_call(functools.partial(kernel, outer, inner), out_shape=jax.Sha...]
where the time goes in v2:
time: 69.5 us; the launch traced here: 69.4 us
  Pallas kernels  66 us (95%)
  local copies, waits for them, and re-layouts  3.27 us (5%)
    pallas_call x1, Pallas kernels, fused(): pl.pallas_call(functools.partial(kernel, outer, inner), out_shape=jax.Sha...  66 us
    unnamed x6, local copies, waits for them, and re-layouts  3.27 us

profile of v2, /device:TPU:0, one launch (start us, length us, event | category | flops | bytes accessed | tf_op | source)
XLA Modules:
  0.0 69.4 jit_solution(739910751113996698)
XLA Ops:
  0.0 0.0 copy-start.1
  0.0 0.0 copy-start
  0.0 1.7 %copy.4 = bf16[256,3,768]{0,2,1:T(8,128)(2,1)S(1)} copy(bf16[256,3,768]{2,0,1:T(8,128)(2,1)} %param.4) | data formatting | bytes 2359296 | tf_op args[1]
  1.7 0.0 copy-done.1
  1.7 0.3 copy-done
  2.0 66.0 %shard_map.37 = f32[768,640]{1,0:T(8,128)S(1)} custom-call(f32[768,640]{1,0:T(8,128)S(1)} %copy-done, bf16[3,768,256]{2,1,0:T(8,128)(2,1)S(1)} %bitcast.1, f32[3,32,512]{2,1,0:T(8,128)S(1)} %copy-done.1), custom_call_target="tpu_custom_call" | custom-call | flops 1509949440 | bytes 3932160 | tf_op jit(solution)/shard_map/pallas_call | solution.py:326
  68.1 1.3 %copy.6 = f32[768,640]{1,0:T(8,128)} copy(f32[768,640]{1,0:T(8,128)S(1)} %shard_map.37) | data formatting | bytes 3932160
Async XLA Ops:
  0.0 1.7 %copy-start.1 = (f32[3,32,512]{2,1,0:T(8,128)S(1)}, f32[3,32,512]{2,1,0:T(8,128)}, u32[]{:S(2)}) copy-start(f32[3,32,512]{2,1,0:T(8,128)} %dinv_ref.1) | copy-start | bytes 589828
  0.0 2.0 %copy-start = (f32[768,640]{1,0:T(8,128)S(1)}, f32[768,640]{1,0:T(8,128)}, u32[]{:S(2)}) copy-start(f32[768,640]{1,0:T(8,128)} %rhs_ref.1) | copy-start | bytes 5898244

commit v3 on v2

--- a/solution.py
+++ b/solution.py
@@ -107,17 +107,17 @@
     far = along_y * (1 - core) + along_x * core
 
     def view(item):
-        kind, i = item
+        kind, lo, hi = item
         if kind == "d":
-            return i, dg.at[core, i]
+            return lo, dg.at[core, lo:hi]
         if kind == "f":
-            return KB + i, fg.at[core, i]
-        return 2 * KB + i, xg.at[i]
+            return KB + lo, fg.at[core, lo:hi]
+        return 2 * KB + lo, xg.at[lo:hi]
 
     def first(item):
-        kind, i = item
+        kind, lo, hi = item
         n, ref = view(item)
-        own = ds.at[i, z] if kind == "d" else ref.at[z, p]
+        own = ds.at[lo:hi, z] if kind == "d" else ref.at[:, z, p]
         copies = []
         for d in range(1, outer):
             c = remote(
@@ -132,7 +132,7 @@
     def in_plane(item, slot, way, to):
         n, ref = view(item)
         c = remote(
-            ref.at[:, slot], ref.at[:, slot], s2_send.at[n, way], s2_recv.at[n, way],
+            ref.at[:, :, slot], ref.at[:, :, slot], s2_send.at[n, way], s2_recv.at[n, way],
             {"row": z * inner + to},
         )
         c.start()
@@ -142,8 +142,8 @@
     def second(item, copies):
         for c in copies:
             c.wait_recv()
-        kind, k = item
-        if kind == "d":
+        kind, lo, hi = item
+        for k in range(lo, hi) if kind == "d" else ():
             for u, ((z0, g0), (z1, g1)) in enumerate(UNITS):
                 dg[core, k, u, p] = ds[k, z0 + core * (z1 - z0), g0 + core * (g1 - g0)]
         return [in_plane(item, p, 0, near), in_plane(item, p, 1, far)]
@@ -173,12 +173,12 @@
             copies.append(c)
         return copies
 
-    order = [("d", 2), ("f", 0), ("d", 1), ("f", 1), ("f", 2), ("d", 0)]
+    order = [("d", 2, 3), ("f", 0, 1), ("d", 1, 2), ("f", 1, 3), ("d", 0, 1)]
+    s2, s1, s0 = ("x", 2, 3), ("x", 1, 2), ("x", 0, 1)
     arrive = {}
     arrive[order[0]] = first(order[0])
     b_copies = all_to_all(bts, btr, 0)
-    for item in order[1:]:
-        arrive[item] = first(item)
+    arrive[order[1]] = first(order[1])
     ft_copy = remote(
         ft_ref, ftx, sib_send.at[2 * KB], sib_recv.at[2 * KB], {"col": 1 - core}
     )
@@ -225,10 +225,13 @@
             total = term if total is None else total + term
         return total
 
-    for item in order[:2]:
-        arrive[item] = second(item, arrive[item])
+    arrive[order[0]] = second(order[0], arrive[order[0]])
+    arrive[order[2]] = first(order[2])
+    arrive[order[1]] = second(order[1], arrive[order[1]])
+    arrive[order[3]] = first(order[3])
     arrive[order[0]] = third(order[0], arrive[order[0]])
     arrive[order[2]] = second(order[2], arrive[order[2]])
+    arrive[order[4]] = first(order[4])
     arrive[order[1]] = third(order[1], arrive[order[1]])
     sib = {}
     sib[order[0]] = to_sibling(order[0], arrive[order[0]])
@@ -239,31 +242,31 @@
     w0 = gathered_rhs(0)
     sib[order[0]].wait_recv()
     x2 = solve(2, w2)
-    a2 = first(("x", 2))
-    for item in order[3:]:
-        arrive[item] = second(item, arrive[item])
-    for item in order[2:]:
-        arrive[item] = third(item, arrive[item])
-    a2 = second(("x", 2), a2)
-    for item in order[1:3]:
-        sib[item] = to_sibling(item, arrive[item])
-    sib[("f", 0)].wait_recv()
+    a2 = first(s2)
+    arrive[order[3]] = second(order[3], arrive[order[3]])
+    arrive[order[2]] = third(order[2], arrive[order[2]])
+    sib[order[1]] = to_sibling(order[1], arrive[order[1]])
+    arrive[order[4]] = second(order[4], arrive[order[4]])
+    a2 = second(s2, a2)
+    sib[order[1]].wait_recv()
     w1 = w1 - couple(0, x2)
-    sib[("d", 1)].wait_recv()
+    sib[order[2]] = to_sibling(order[2], arrive[order[2]])
+    arrive[order[3]] = third(order[3], arrive[order[3]])
+    sib[order[2]].wait_recv()
     x1 = solve(1, w1)
-    a1 = first(("x", 1))
-    for item in order[3:]:
-        sib[item] = to_sibling(item, arrive[item])
-    a2 = third(("x", 2), a2)
-    a1 = second(("x", 1), a1)
-    sib[("f", 1)].wait_recv()
+    a1 = first(s1)
+    arrive[order[4]] = third(order[4], arrive[order[4]])
+    sib[order[3]] = to_sibling(order[3], arrive[order[3]])
+    a2 = third(s2, a2)
+    sib[order[3]].wait_recv()
     w0 = w0 - couple(1, x2)
-    sib[("f", 2)].wait_recv()
     w0 = w0 - couple(2, x1)
-    sib[("d", 0)].wait_recv()
+    a1 = second(s1, a1)
+    sib[order[4]] = to_sibling(order[4], arrive[order[4]])
+    sib[order[4]].wait_recv()
     x0 = solve(0, w0)
-    a0 = first(("x", 0))
-    a1 = third(("x", 1), a1)
+    a0 = first(s0)
+    a1 = third(s1, a1)
 
     whole = [jnp.concatenate(x, axis=1) for x in (x0, x1, x2)]
     for r in range(n_row):
@@ -278,8 +281,8 @@
             total = jnp.where(lane_group == start // block, part, total)
         yts[r] = total
     ytr[me] = yts[me]
+    a0 = second(s0, a0)
     y_copies = all_to_all(yts, ytr, 1)
-    a0 = second(("x", 0), a0)
 
     tiles = 3
     tile = kept // tiles
@@ -302,7 +305,7 @@
 
     ft_copy.wait_recv()
     update(2, a2, rhs_ref)
-    a0 = third(("x", 0), a0)
+    a0 = third(s0, a0)
     update(1, a1, out_ref)
     update(0, a0, out_ref)
     for c in y_copies:

time: 69.5 us -> 66.9 us (0.963)
  Pallas kernels: 66 us -> 63.4 us
    pallas_call x1, Pallas kernels: 66 us -> 63.4 us  [fused(): pl.pallas_call(functools.partial(kernel, outer, inner), out_shape=jax.Sha...]
where the time goes in v3:
time: 66.9 us; the launch traced here: 66.7 us
  Pallas kernels  63.4 us (95%)
  local copies, waits for them, and re-layouts  3.27 us (5%)
    pallas_call x1, Pallas kernels, fused(): pl.pallas_call(functools.partial(kernel, outer, inner), out_shape=jax.Sha...  63.4 us
    unnamed x6, local copies, waits for them, and re-layouts  3.27 us

profile of v3, /device:TPU:0, one launch (start us, length us, event | category | flops | bytes accessed | tf_op | source)
XLA Modules:
  0.0 66.7 jit_solution(9656809002314206951)
XLA Ops:
  0.0 0.0 copy-start.1
  0.0 0.0 copy-start
  0.0 1.7 %copy.4 = bf16[256,3,768]{0,2,1:T(8,128)(2,1)S(1)} copy(bf16[256,3,768]{2,0,1:T(8,128)(2,1)} %param.4) | data formatting | bytes 2359296 | tf_op args[1]
  1.7 0.0 copy-done.1
  1.7 0.3 copy-done
  2.0 63.4 %shard_map.37 = f32[768,640]{1,0:T(8,128)S(1)} custom-call(f32[768,640]{1,0:T(8,128)S(1)} %copy-done, bf16[3,768,256]{2,1,0:T(8,128)(2,1)S(1)} %bitcast.1, f32[3,32,512]{2,1,0:T(8,128)S(1)} %copy-done.1), custom_call_target="tpu_custom_call" | custom-call | flops 1509949440 | bytes 3932160 | tf_op jit(solution)/shard_map/pallas_call | solution.py:329
  65.5 1.3 %copy.6 = f32[768,640]{1,0:T(8,128)} copy(f32[768,640]{1,0:T(8,128)S(1)} %shard_map.37) | data formatting | bytes 3932160
Async XLA Ops:
  0.0 1.7 %copy-start.1 = (f32[3,32,512]{2,1,0:T(8,128)S(1)}, f32[3,32,512]{2,1,0:T(8,128)}, u32[]{:S(2)}) copy-start(f32[3,32,512]{2,1,0:T(8,128)} %dinv_ref.1) | copy-start | bytes 589828
  0.0 2.0 %copy-start = (f32[768,640]{1,0:T(8,128)S(1)}, f32[768,640]{1,0:T(8,128)}, u32[]{:S(2)}) copy-start(f32[768,640]{1,0:T(8,128)} %rhs_ref.1) | copy-start | bytes 5898244

commit v4 on v3

--- a/solution.py
+++ b/solution.py
@@ -268,6 +268,25 @@
     a0 = first(s0)
     a1 = third(s1, a1)
 
+    tiles = 3
+    tile = kept // tiles
+
+    def update(k, copies, base):
+        for c in copies:
+            c.wait_recv()
+        v = xg[k].reshape(n_row, 2 * chunk, half).astype(jnp.float32)
+        for h in range(2):
+            xt[h] = v[:, h * chunk : (h + 1) * chunk].reshape(n_row * chunk, half).astype(
+                jnp.bfloat16
+            )
+
+        @pl.loop(0, tiles)
+        def _(t):
+            at = pl.ds(pl.multiple_of(t * tile, tile), tile)
+            out_ref[at, :] = (
+                base[at, :] - nt_dot(ft_ref[k, at, :], xt[core]) - nt_dot(ftx[k, at, :], xt[1 - core])
+            )
+
     whole = [jnp.concatenate(x, axis=1) for x in (x0, x1, x2)]
     for r in range(n_row):
         g, q = r // per_tile, r % per_tile
@@ -281,30 +300,11 @@
             total = jnp.where(lane_group == start // block, part, total)
         yts[r] = total
     ytr[me] = yts[me]
+    ft_copy.wait_recv()
+    update(2, a2, rhs_ref)
     a0 = second(s0, a0)
     y_copies = all_to_all(yts, ytr, 1)
 
-    tiles = 3
-    tile = kept // tiles
-
-    def update(k, copies, base):
-        for c in copies:
-            c.wait_recv()
-        v = xg[k].reshape(n_row, 2 * chunk, half).astype(jnp.float32)
-        for h in range(2):
-            xt[h] = v[:, h * chunk : (h + 1) * chunk].reshape(n_row * chunk, half).astype(
-                jnp.bfloat16
-            )
-
-        @pl.loop(0, tiles)
-        def _(t):
-            at = pl.ds(pl.multiple_of(t * tile, tile), tile)
-            out_ref[at, :] = (
-                base[at, :] - nt_dot(ft_ref[k, at, :], xt[core]) - nt_dot(ftx[k, at, :], xt[1 - core])
-            )
-
-    ft_copy.wait_recv()
-    update(2, a2, rhs_ref)
     a0 = third(s0, a0)
     update(1, a1, out_ref)
     update(0, a0, out_ref)

time: 66.9 us -> 67.1 us (level)
  no operation moved by 1% of the time
where the time goes in v4:
time: 67.1 us; the launch traced here: 66.9 us
  Pallas kernels  63.6 us (95%)
  local copies, waits for them, and re-layouts  3.27 us (5%)
    pallas_call x1, Pallas kernels, fused(): pl.pallas_call(functools.partial(kernel, outer, inner), out_shape=jax.Sha...  63.6 us
    unnamed x6, local copies, waits for them, and re-layouts  3.27 us

profile of v4, /device:TPU:0, one launch (start us, length us, event | category | flops | bytes accessed | tf_op | source)
XLA Modules:
  0.0 66.9 jit_solution(13751520791442298713)
XLA Ops:
  0.0 0.0 copy-start.1
  0.0 0.0 copy-start
  0.0 1.7 %copy.4 = bf16[256,3,768]{0,2,1:T(8,128)(2,1)S(1)} copy(bf16[256,3,768]{2,0,1:T(8,128)(2,1)} %param.4) | data formatting | bytes 2359296 | tf_op args[1]
  1.7 0.0 copy-done.1
  1.7 0.3 copy-done
  2.0 63.6 %shard_map.37 = f32[768,640]{1,0:T(8,128)S(1)} custom-call(f32[768,640]{1,0:T(8,128)S(1)} %copy-done, bf16[3,768,256]{2,1,0:T(8,128)(2,1)S(1)} %bitcast.1, f32[3,32,512]{2,1,0:T(8,128)S(1)} %copy-done.1), custom_call_target="tpu_custom_call" | custom-call | flops 1509949440 | bytes 3932160 | tf_op jit(solution)/shard_map/pallas_call | solution.py:329
  65.6 1.3 %copy.6 = f32[768,640]{1,0:T(8,128)} copy(f32[768,640]{1,0:T(8,128)S(1)} %shard_map.37) | data formatting | bytes 3932160
Async XLA Ops:
  0.0 1.7 %copy-start.1 = (f32[3,32,512]{2,1,0:T(8,128)S(1)}, f32[3,32,512]{2,1,0:T(8,128)}, u32[]{:S(2)}) copy-start(f32[3,32,512]{2,1,0:T(8,128)} %dinv_ref.1) | copy-start | bytes 589828
  0.0 2.0 %copy-start = (f32[768,640]{1,0:T(8,128)S(1)}, f32[768,640]{1,0:T(8,128)}, u32[]{:S(2)}) copy-start(f32[768,640]{1,0:T(8,128)} %rhs_ref.1) | copy-start | bytes 5898244
